TPU v7x, 32 devices: a whole 2x2x4 slice. The times are simulated.
32 devices in a mesh: slab: 16 (over z, y, x), grp: 2 (over core).
Axes of the slice: x: 2, y: 2, z: 4, core: 2. Of those that a mesh axis runs over, the one named last changes fastest.
Arguments:
- echo_data: bfloat16 [16, 1024, 2048], P('slab', 'grp'), may hold values from -6 to 6
- acquirer: int32 [3], replicated, may hold values from 0 to 15, as said below
- panels: bfloat16 [16, 3, 64, 128, 128], P('slab', None, 'grp'), may hold values from -0.00390625 to 0.00390625
- block_count: int32 [16, 3], P('slab'), may hold values from 16 to 64, as said below
- block_rows: int32 [16, 3, 64], P('slab'), may hold values from 0 to 7
- block_columns: int32 [16, 3, 64], P('slab'), may hold values from 0 to 15
- apodization: float32 [16, 1024], P(None, 'grp'), may hold values from 0.25 to 2.5
- window_index: int32 [16384], P('slab'), may hold values from 0 to 15
Outputs:
- image: float32 [16384], P(('slab', 'grp'))
Inputs may be any that keep to these rules, and one draw needn't show every extreme that they name: `acquirer`: 3 distinct slab indices, the last slab index always among them. `block_count`: slots below the count are live, the others unused; some slab and transmit has all 64 live in every draw.
All inputs are finite; a program needn't handle non-finite values.
Results may differ from a plain program's by a relative error of at most 0.0003.
Values may be sent and summed in bfloat16 or wider, within the bound.
A program may use at most 128 MiB of HBM per device.

v0:
```python
import math

import jax
import jax.numpy as jnp
from jax import lax
from jax.sharding import PartitionSpec as P


def from_root(block, axis, holder):
    block = jnp.where(lax.axis_index(axis) == holder, block, jnp.zeros_like(block))
    return lax.psum(block, axis)


def table_rows(window_index, table):
    windows = table.shape[0]
    onehot = (window_index[:, None] == jnp.arange(windows, dtype=jnp.int32)[None, :]).astype(
        jnp.float32
    )
    return jnp.dot(
        onehot, table, precision=lax.Precision.HIGHEST, preferred_element_type=jnp.float32
    )


def block_terms(piece, columns, signal):
    block_size = piece.shape[-1]
    channels = signal.shape[0]
    grid = signal.reshape(channels, signal.shape[1] // block_size, block_size)
    picked = jnp.take(grid, columns, axis=1)
    return jnp.einsum("kvs,cks->kvc", piece, picked, preferred_element_type=jnp.float32)


def place_rows(terms, rows, live, row_blocks):
    onehot = (rows[:, None] == jnp.arange(row_blocks, dtype=jnp.int32)[None, :]).astype(
        jnp.float32
    ) * live[:, None]
    return jnp.einsum("kr,kvc->rvc", onehot, terms, precision=lax.Precision.HIGHEST)


def masked_slots(running, piece, rows, columns, live, signal):
    width = piece.shape[0]
    block_size = piece.shape[-1]
    channels = signal.shape[0]
    limit = max(1, (1 << 18) // (block_size * channels))
    group = math.gcd(width, limit)
    turns = width // group
    grouped = (
        piece.reshape(turns, group, block_size, block_size),
        rows.reshape(turns, group),
        columns.reshape(turns, group),
        live.reshape(turns, group),
    )

    def one_group(current, inputs):
        group_piece, group_rows, group_columns, group_live = inputs
        terms = block_terms(group_piece, group_columns, signal)
        return (current + place_rows(terms, group_rows, group_live, current.shape[0]), None)

    result, unused = lax.scan(one_group, running, grouped)
    return result


def add_slots(running, piece, rows_all, columns_all, count, signal):
    width = piece.shape[0]
    live = (jnp.arange(width, dtype=jnp.int32) < count).astype(jnp.float32)
    return masked_slots(running, piece, rows_all, columns_all, live, signal)


def per_device(
    echo_data, acquirer, panels, block_count, block_rows, block_columns, apodization, window_index
):
    signal_own = echo_data[0]
    block_size = panels.shape[-1]
    voxel_count = window_index.shape[0]
    row_blocks = voxel_count // block_size
    weights = table_rows(window_index, apodization)
    running = jnp.zeros((row_blocks, block_size, signal_own.shape[0]), jnp.float32)
    for transmit in range(acquirer.shape[0]):
        signal = from_root(signal_own, "slab", acquirer[transmit])
        rows_all = block_rows[0, transmit]
        columns_all = block_columns[0, transmit]
        count = block_count[0, transmit]

        def fold_panels(
            current,
            piece,
            start,
            signal=signal,
            rows_all=rows_all,
            columns_all=columns_all,
            count=count,
        ):
            return add_slots(current, piece, rows_all, columns_all, count, signal)

        running = fold_panels(
            running, lax.all_gather(panels[0, transmit], "grp", axis=0, tiled=True), jnp.int32(0)
        )
    partial_value = jnp.sum(running.reshape(voxel_count, running.shape[2]) * weights, axis=1)
    return lax.psum_scatter(partial_value, "grp", scatter_dimension=0, tiled=True)


def solution(mesh):
    return jax.shard_map(
        per_device,
        mesh=mesh,
        in_specs=(
            P("slab", "grp", None),
            P(),
            P("slab", None, "grp", None, None),
            P("slab", None),
            P("slab", None, None),
            P("slab", None, None),
            P(None, "grp"),
            P("slab"),
        ),
        out_specs=P(("slab", "grp")),
        check_vma=False,
    )
```

profile of v0, /device:TPU:0, one launch (start us, length us, event | category | flops | bytes accessed | tf_op | source)
XLA Modules:
  0.0 789.7 jit_solution(2284421754817701473)
XLA Ops:
  25.6 207.8 %all-reduce.4.cloned.1.call-done = (bf16[512,2048]{0,1:T(8,128)(2,1)}, bf16[512,2048]{0,1:T(8,128)(2,1)}, bf16[512,2048]{0,1:T(8,128)(2,1)}) async-done(((bf16[512,2048]{0,1:T(8,128)(2,1)}, bf16[512,2048]{0,1:T(8,128)(2,1)}, bf16[512,2048]{0,1:T(8,128)(2,1)}), (bf16[512,2048]{0,1:T(8,128)(2,1)}, bf16[512,2048]{0,1:T(8,128)(2,1)}, bf16[512,2048]{0,1:T(8,128)(2,1)})) %all-reduce.4.cloned.1.call-update) | async-done | bytes 6291472 | tf_op jit(solution)/shard_map/psum | solution.py:11
  233.4 187.9 %while.33 = (s32[]{:T(128)}, f32[8,128,512]{2,0,1:T(8,128)S(1)}, s32[16,4]{1,0:T(8,128)S(1)}, f32[16,4]{1,0:T(8,128)S(1)}, bf16[16,4,128,128]{3,2,1,0:T(8,128)(2...) while((s32[]{:T(128)}, f32[8,128,512]{2,0,1:T(8,128)S(1)}, ...), condition=%wide.region_2.4_spmd.clone, body=%wide.region_1.3_spmd.clone.sunk | while | flops 93586520 | bytes 12194587 | solution.py:58
  233.4 3.9 copy.56
  245.2 3.9 copy.56
  256.9 3.9 copy.56
  268.6 3.9 copy.56
  280.4 3.9 copy.56
  292.1 3.9 copy.56
  303.9 3.9 copy.56
  315.6 3.9 copy.56
  327.4 3.9 copy.56
  339.1 3.9 copy.56
  350.8 3.9 copy.56
  362.6 3.9 copy.56
  374.3 3.9 copy.56
  386.1 3.9 copy.56
  397.8 3.9 copy.56
  409.6 3.9 copy.56
  421.3 176.4 %while.31 = (s32[]{:T(128)}, f32[8,128,512]{2,0,1:T(8,128)S(1)}, s32[16,4]{1,0:T(8,128)S(1)}, f32[16,4]{1,0:T(8,128)S(1)}, bf16[16,4,128,128]{3,2,1,0:T(8,128)(2...) while((s32[]{:T(128)}, f32[8,128,512]{2,0,1:T(8,128)S(1)}, s32[16,4]{1,0:T(8,128)S(1)}, ...), condition=%wide.region_5.7_spmd, body=%wide.region_4.6_spmd.sunk | while | flops 93062232 | bytes 12194569 | solution.py:58
  421.3 3.9 copy.52
  432.4 3.9 copy.52
  443.4 3.9 copy.52
  454.4 3.9 copy.52
  465.4 3.9 copy.52
  476.5 3.9 copy.52
  487.5 3.9 copy.52
  498.5 3.9 copy.52
  509.5 3.9 copy.52
  520.6 3.9 copy.52
  575.7 3.9 copy.52
  586.7 3.9 copy.52
  597.7 176.6 %while.32 = (s32[]{:T(128)}, f32[8,128,512]{2,0,1:T(8,128)S(1)}, s32[16,4]{1,0:T(8,128)S(1)}, f32[16,4]{1,0:T(8,128)S(1)}, bf16[16,4,128,128]{3,2,1,0:T(8,128)(2...) while((s32[]{:T(128)}, f32[8,128,512]{2,0,1:T(8,128)S(1)}, s32[16,4]{1,0:T(8,128)S(1)}, ...), condition=%wide.region_8.10_spmd, body=%wide.region_7.9_spmd.sunk | while | flops 93062232 | bytes 12194569 | solution.py:58
  598.0 3.9 copy.54
  609.0 3.9 copy.54
  620.0 3.9 copy.54
  631.0 3.9 copy.54
  642.1 3.9 copy.54
  653.1 3.9 copy.54
  664.1 3.9 copy.54
  675.1 3.9 copy.54
  686.2 3.9 copy.54
  697.2 3.9 copy.54
  708.2 3.9 copy.54
  719.2 3.9 copy.54
  730.2 3.9 copy.54
  741.3 3.9 copy.54
  752.3 3.9 copy.54
  763.3 3.9 copy.54
  (386 shorter events, 389.8 us)
Async XLA Ops:
  7.4 769.0 %copy-start = (f32[16,512]{1,0:T(8,128)S(1)}, f32[16,512]{1,0:T(8,128)}, u32[]{:S(2)}) copy-start(f32[16,512]{1,0:T(8,128)} %param.22) | copy-start | bytes 98308
  7.4 3.7 copy-start.1
  7.4 18.2 %all-gather.7.cloned.1.call-start = ((), (), s32[]{:S(2)}) async-start(), calls=%async_computation | async-start | bytes 3145728 | tf_op jit(solution)/shard_map/all_gather | solution.py:95
  11.1 222.3 %all-reduce.4.cloned.1.call-start = ((), (), s32[]{:S(2)}) async-start(), calls=%async_computation.3 | async-start | bytes 12582912 | tf_op jit(solution)/shard_map/psum | solution.py:11
  19.4 1.6 copy-start.4
  19.5 1.6 copy-start.5
  19.5 1.7 copy-start.2
  19.5 4.7 copy-start.6
  19.5 401.8 %all-gather.9.cloned.1.call-start = ((), (), s32[]{:S(2)}) async-start(), calls=%async_computation.1 | async-start | bytes 3145728 | tf_op jit(solution)/shard_map/all_gather | solution.py:95
  20.2 577.5 %all-gather.11.cloned.1.call-start = ((), (), s32[]{:S(2)}) async-start(), calls=%async_computation.2 | async-start | bytes 3145728 | tf_op jit(solution)/shard_map/all_gather | solution.py:95
  774.3 2.1 copy-start.3
Sparse Core Ops, SparseCore 0:
  11.2 13.2 all-gather.6
  26.0 11.7 all-gather.8
  39.4 11.7 all-gather.10
Sparse Core Ops, SparseCore 1:
  19.5 213.8 all-reduce.3
where the time goes:
time: 795 us; the launch traced here: 790 us
  local copies, waits for them, and re-layouts  320 us (40%)
  matrix products  231 us (29%)
  waiting for transfers between devices  209 us (26%)
  between operations  17.4 us (2%)
    psum x1, waiting for transfers between devices, from_root(): return lax.psum(block, axis)  208 us
    reshape x48, local copies, waits for them, and re-layouts, block_terms(): grid = signal.reshape(channels, signal.shape[1] // block_size, block_size)  187 us
    dot_general x48, matrix products, place_rows(): jnp.einsum('kr,kvc->rvc', onehot, terms, precision=lax.Precision.HIGHEST)  164 us
    gather x48, local copies, waits for them, and re-layouts, block_terms(): picked = jnp.take(grid, columns, axis=1)  120 us
    dot_general x48, matrix products, block_terms(): jnp.einsum('kvs,cks->kvc', piece, picked, preferred_element_type=jnp.floa...  64.8 us
  transfers between devices with their start and end apart: 4, of which 1 were waited for; matrix products, arithmetic and copies ran while one was open for 47% of the time, Pallas kernels for 0%

commit v1 on v0

v1 whole, which is shorter than its diff:
```python
import functools

import jax
import jax.numpy as jnp
from jax import lax
from jax.experimental import pallas as pl
from jax.experimental.pallas import tpu as pltpu
from jax.sharding import PartitionSpec as P

MESH = pl.DeviceIdType.MESH
F32 = jnp.float32
BF16 = jnp.bfloat16
LANES = 128


def split_terms(x, n):
    terms = []
    for _ in range(n):
        term = x.astype(BF16)
        terms.append(term)
        x = x - term.astype(F32)
    return terms


def kernel(
    dims,
    echo,
    panels,
    apod,
    windows,
    acquirer,
    counts,
    rows,
    columns,
    image,
    echo_v,
    panels_v,
    own,
    parts,
    line,
    table,
    onehot,
    sums,
    echo_sem,
    panel_sem,
    send1,
    recv1,
    send2,
    recv2,
    send3,
    recv3,
    send4,
    recv4,
):
    n_grp, plane, n_lines, n_tx, n_win, piece, width, unroll = dims
    peers = plane * n_grp
    span = piece * LANES
    slab, grp = lax.axis_index("slab"), lax.axis_index("grp")
    level, spot = slab // plane, slab % plane
    me = spot * n_grp + grp

    def peer(step):
        other = lax.rem(me + step, peers)
        return other, (level * plane + other // n_grp, lax.rem(other, n_grp))

    def along(step):
        other = lax.rem(level + step, n_lines)
        return other, (other * plane + spot, grp)

    def sibling(step):
        other = lax.rem(grp + step, n_grp)
        return other, (slab, other)

    barrier = pltpu.get_barrier_semaphore()
    for step in range(1, peers):
        pl.semaphore_signal(barrier, inc=1, device_id=peer(step)[1], device_id_type=MESH)
    for step in range(1, n_lines):
        pl.semaphore_signal(barrier, inc=1, device_id=along(step)[1], device_id_type=MESH)

    order = [lax.rem(me + step, peers) for step in range(1, peers + 1)]
    loads = []
    for number, part in enumerate(order):
        cut = pl.ds(pl.multiple_of(part * span, span), span)
        load = pltpu.make_async_copy(echo.at[0, :, cut], echo_v.at[number], echo_sem.at[number])
        load.start()
        loads.append(load)
    panel_loads = []
    for t in range(n_tx):
        load = pltpu.make_async_copy(panels.at[0, t], panels_v.at[t], panel_sem.at[t])
        load.start()
        panel_loads.append(load)

    row_blocks = windows.shape[0]
    for r in range(row_blocks):
        ids = lax.broadcasted_iota(jnp.int32, (n_win, LANES), 0)
        onehot[r] = jnp.where(ids == windows[r : r + 1, :], 1.0, 0.0).astype(F32)

    weights = jnp.concatenate(split_terms(apod[...], 3), axis=0)

    pl.semaphore_wait(barrier, peers - 1 + n_lines - 1)

    copies = []
    for number, part in enumerate(order):
        loads[number].wait()
        terms = jnp.dot(weights, echo_v[number], preferred_element_type=F32)
        value = terms[:n_win] + terms[n_win : 2 * n_win] + terms[2 * n_win :]
        for c in range(piece):
            chunk = value[:, c * LANES : (c + 1) * LANES]
            if number == peers - 1:
                parts[me, c] = chunk
            else:
                own[number, c] = chunk
        if number < peers - 1:
            copy = pltpu.make_async_remote_copy(
                src_ref=own.at[number],
                dst_ref=parts.at[me],
                send_sem=send1.at[number],
                recv_sem=recv1.at[me],
                device_id=peer(number + 1)[1],
                device_id_type=MESH,
            )
            copy.start()
            copies.append(copy)
    for step in range(1, peers):
        other, place = peer(step)
        pltpu.make_async_remote_copy(
            src_ref=own.at[0],
            dst_ref=parts.at[other],
            send_sem=send1.at[0],
            recv_sem=recv1.at[other],
            device_id=place,
            device_id_type=MESH,
        ).wait_recv()

    for c in range(piece):
        records = []
        for q in range(plane):
            total = parts[q * n_grp, c]
            for g in range(1, n_grp):
                total = total + parts[q * n_grp + g, c]
            records.append(total)
        for t in range(n_tx):
            value = jnp.zeros((n_win, LANES), F32)
            for q in range(plane):
                hit = jnp.full((n_win, LANES), acquirer[t], jnp.int32) == level * plane + q
                value = value + jnp.where(hit, records[q], 0.0)
            line[level, c, t] = value
    for step in range(1, n_lines):
        other, place = along(step)
        copy = pltpu.make_async_remote_copy(
            src_ref=line.at[level],
            dst_ref=line.at[level],
            send_sem=send2.at[step],
            recv_sem=recv2.at[level],
            device_id=place,
            device_id_type=MESH,
        )
        copy.start()
        copies.append(copy)
    for step in range(1, n_lines):
        other, place = along(step)
        pltpu.make_async_remote_copy(
            src_ref=line.at[other],
            dst_ref=line.at[other],
            send_sem=send2.at[step],
            recv_sem=recv2.at[other],
            device_id=place,
            device_id_type=MESH,
        ).wait_recv()

    mine = pl.ds(me * piece, piece)
    for c in range(piece):
        for t in range(n_tx):
            value = line[0, c, t]
            for l in range(1, n_lines):
                value = value + line[l, c, t]
            table[me * piece + c, t] = jnp.concatenate(split_terms(value, 2), axis=0)
    for step in range(1, peers):
        other, place = peer(step)
        copy = pltpu.make_async_remote_copy(
            src_ref=table.at[mine],
            dst_ref=table.at[mine],
            send_sem=send3.at[step],
            recv_sem=recv3.at[me],
            device_id=place,
            device_id_type=MESH,
        )
        copy.start()
        copies.append(copy)
    for step in range(1, peers):
        other, place = peer(step)
        theirs = pl.ds(other * piece, piece)
        pltpu.make_async_remote_copy(
            src_ref=table.at[theirs],
            dst_ref=table.at[theirs],
            send_sem=send3.at[step],
            recv_sem=recv3.at[other],
            device_id=place,
            device_id_type=MESH,
        ).wait_recv()

    row_ids = lax.broadcasted_iota(jnp.int32, (row_blocks, LANES), 0)
    acc = jnp.zeros((row_blocks, LANES), F32)
    for t in range(n_tx):
        panel_loads[t].wait()

        def some_slots(turn, acc, t=t):
            for u in range(unroll):
                k = turn * unroll + u
                slot = grp * width + k
                r = rows[t, 0, slot]
                signal = table[columns[t, 0, slot], t]
                both = lax.dot_general(
                    signal,
                    panels_v[t, k],
                    (((1,), (1,)), ((), ())),
                    preferred_element_type=F32,
                )
                value = (both[:n_win] + both[n_win:]) * onehot[r]
                value = jnp.sum(value, axis=0, keepdims=True)
                target = jnp.where(slot < counts[0, t], r, -1)
                acc = acc + jnp.where(row_ids == target, value, 0.0)
            return acc

        acc = lax.fori_loop(0, width // unroll, some_slots, acc)

    sums[grp] = acc
    for step in range(1, n_grp):
        other, place = sibling(step)
        copy = pltpu.make_async_remote_copy(
            src_ref=sums.at[grp],
            dst_ref=sums.at[grp],
            send_sem=send4.at[step],
            recv_sem=recv4.at[grp],
            device_id=place,
            device_id_type=MESH,
        )
        copy.start()
        copies.append(copy)
    for step in range(1, n_grp):
        other, place = sibling(step)
        pltpu.make_async_remote_copy(
            src_ref=sums.at[other],
            dst_ref=sums.at[other],
            send_sem=send4.at[step],
            recv_sem=recv4.at[other],
            device_id=place,
            device_id_type=MESH,
        ).wait_recv()
    total = sums[0]
    for g in range(1, n_grp):
        total = total + sums[g]
    share = row_blocks // n_grp
    result = total[:share]
    for g in range(1, n_grp):
        result = jnp.where(grp == g, total[g * share : (g + 1) * share], result)
    image[...] = result
    for copy in copies:
        copy.wait_send()


def per_device(
    n_slab,
    n_grp,
    echo_data,
    acquirer,
    panels,
    block_count,
    block_rows,
    block_columns,
    apodization,
    window_index,
):
    channels, samples = echo_data.shape[1:]
    n_tx, width, block = panels.shape[1:4]
    n_win = apodization.shape[0]
    n_blocks = samples // block
    row_blocks = window_index.shape[0] // block
    plane = min(4, n_slab, n_blocks // n_grp)
    n_lines = n_slab // plane
    peers = plane * n_grp
    piece = n_blocks // peers
    assert block == LANES and piece * peers == n_blocks and plane * n_lines == n_slab
    unroll = min(8, width)
    dims = (n_grp, plane, n_lines, n_tx, n_win, piece, width, unroll)
    vmem = pl.BlockSpec(memory_space=pltpu.VMEM)
    smem = pl.BlockSpec(memory_space=pltpu.SMEM)
    hbm = pl.BlockSpec(memory_space=pltpu.HBM)
    dma = pltpu.SemaphoreType.DMA
    result = pl.pallas_call(
        functools.partial(kernel, dims),
        out_shape=jax.ShapeDtypeStruct((row_blocks // n_grp, LANES), F32),
        in_specs=[hbm, hbm, vmem, vmem, smem, smem, smem, smem],
        out_specs=vmem,
        scratch_shapes=[
            pltpu.VMEM((peers, channels, piece * LANES), BF16),
            pltpu.VMEM((n_tx, width, block, block), BF16),
            pltpu.VMEM((peers, piece, n_win, LANES), F32),
            pltpu.VMEM((peers, piece, n_win, LANES), F32),
            pltpu.VMEM((n_lines, piece, n_tx, n_win, LANES), F32),
            pltpu.VMEM((n_blocks, n_tx, 2 * n_win, LANES), BF16),
            pltpu.VMEM((row_blocks, n_win, LANES), F32),
            pltpu.VMEM((n_grp, row_blocks, LANES), F32),
            dma((peers,)),
            dma((n_tx,)),
            dma((peers,)),
            dma((peers,)),
            dma((n_lines,)),
            dma((n_lines,)),
            dma((peers,)),
            dma((peers,)),
            dma((n_grp,)),
            dma((n_grp,)),
        ],
        compiler_params=pltpu.CompilerParams(
            collective_id=0, has_side_effects=True, vmem_limit_bytes=62 * 1024 * 1024
        ),
        name="beamform",
    )(
        echo_data,
        panels,
        apodization,
        window_index.reshape(row_blocks, block),
        acquirer,
        block_count,
        block_rows.transpose(1, 0, 2),
        block_columns.transpose(1, 0, 2),
    )
    return result.reshape(-1)


def solution(mesh):
    return jax.shard_map(
        functools.partial(per_device, mesh.shape["slab"], mesh.shape["grp"]),
        mesh=mesh,
        in_specs=(
            P("slab", "grp", None),
            P(),
            P("slab", None, "grp", None, None),
            P("slab", None),
            P("slab", None, None),
            P("slab", None, None),
            P(None, "grp"),
            P("slab"),
        ),
        out_specs=P(("slab", "grp")),
        check_vma=False,
    )
```

time: 795 us -> 27.7 us (0.03)
  local copies, waits for them, and re-layouts: 320 us -> 1.26 us
  matrix products: 231 us -> 0 us
  waiting for transfers between devices: 209 us -> 0 us
  Pallas kernels: 0 us -> 26.2 us
  between operations: 17.4 us -> 0.01 us
    dot_general x97 -> x0, matrix products: 231 us -> none  [the longest x48 164 us: place_rows(): jnp.einsum('kr,kvc->rvc', onehot, terms, precision=lax.Precision.HIGHEST)]
    psum x1 -> x0, waiting for transfers between devices: 208 us -> none  [from_root(): return lax.psum(block, axis)]
    reshape x48 -> x0, local copies, waits for them, and re-layouts: 187 us -> none  [block_terms(): grid = signal.reshape(channels, signal.shape[1] // block_size, block_size)]
    gather x48 -> x0, local copies, waits for them, and re-layouts: 120 us -> none  [block_terms(): picked = jnp.take(grid, columns, axis=1)]
    pallas_call x0 -> x1, Pallas kernels: none -> 26.2 us  [per_device(): pl.pallas_call(functools.partial(kernel, dims), out_shape=jax.ShapeDtypeS...]
  transfers between devices with their start and end apart: 4 -> 0, of which waited for: 1 -> 0; matrix products, arithmetic and copies ran while one was open for 47% -> 0% of each run, Pallas kernels for 0% -> 0%
where the time goes in v1:
time: 27.7 us; the launch traced here: 27.5 us
  Pallas kernels  26.2 us (95%)
  local copies, waits for them, and re-layouts  1.26 us (5%)
    pallas_call x1, Pallas kernels, per_device(): pl.pallas_call(functools.partial(kernel, dims), out_shape=jax.ShapeDtypeS...  26.2 us
    unnamed x1, local copies, waits for them, and re-layouts  1.26 us

profile of v1, /device:TPU:0, one launch (start us, length us, event | category | flops | bytes accessed | tf_op | source)
XLA Modules:
  0.0 27.5 jit_solution(7384101388324886882)
XLA Ops:
  0.0 26.2 %beamform.1 = f32[4,128]{1,0:T(4,128)} custom-call(bf16[1,512,2048]{2,1,0:T(8,128)(2,1)} %echo.1, bf16[1,3,32,128,128]{4,3,2,1,0:T(8,128)(2,1)} %panels.1, f32[16,512]{1,0:T(8,128)} %apod.1, s32[8,128]{1,0:T(8,128)} %bitcast.5, s32[3]{0:T(128)} %acquirer.1, s32[1,3]{1,0:T(1,128)} %counts.1, s32[3,1,64]{2,1,0:T(1,128)} %bitcast.6, s32[3,1,64]{2,1,0:T(1,128)} %bitcast.7), custom_call_target="tpu_custom_call" | custom-call | tf_op jit(solution)/shard_map/beamform/pallas_call | solution.py:290
  26.2 1.3 %copy.10 = f32[512]{0:T(512)} copy(f32[512]{0:T(512)} %bitcast.4) | data formatting | bytes 4096

commit v2 on v1

--- a/solution.py
+++ b/solution.py
@@ -38,7 +38,7 @@
     own,
     parts,
     line,
-    table,
+    tables,
     onehot,
     sums,
     echo_sem,
@@ -132,84 +132,85 @@
             device_id_type=MESH,
         ).wait_recv()
 
+    records = []
     for c in range(piece):
-        records = []
         for q in range(plane):
             total = parts[q * n_grp, c]
             for g in range(1, n_grp):
                 total = total + parts[q * n_grp + g, c]
             records.append(total)
-        for t in range(n_tx):
+    for t in range(n_tx):
+        for c in range(piece):
             value = jnp.zeros((n_win, LANES), F32)
             for q in range(plane):
                 hit = jnp.full((n_win, LANES), acquirer[t], jnp.int32) == level * plane + q
-                value = value + jnp.where(hit, records[q], 0.0)
-            line[level, c, t] = value
-    for step in range(1, n_lines):
-        other, place = along(step)
-        copy = pltpu.make_async_remote_copy(
-            src_ref=line.at[level],
-            dst_ref=line.at[level],
-            send_sem=send2.at[step],
-            recv_sem=recv2.at[level],
-            device_id=place,
-            device_id_type=MESH,
-        )
-        copy.start()
-        copies.append(copy)
-    for step in range(1, n_lines):
-        other, place = along(step)
-        pltpu.make_async_remote_copy(
-            src_ref=line.at[other],
-            dst_ref=line.at[other],
-            send_sem=send2.at[step],
-            recv_sem=recv2.at[other],
-            device_id=place,
-            device_id_type=MESH,
-        ).wait_recv()
+                value = value + jnp.where(hit, records[c * plane + q], 0.0)
+            line[level, t, c] = value
+        for step in range(1, n_lines):
+            other, place = along(step)
+            copy = pltpu.make_async_remote_copy(
+                src_ref=line.at[level, t],
+                dst_ref=line.at[level, t],
+                send_sem=send2.at[t, step],
+                recv_sem=recv2.at[t, level],
+                device_id=place,
+                device_id_type=MESH,
+            )
+            copy.start()
+            copies.append(copy)
 
     mine = pl.ds(me * piece, piece)
-    for c in range(piece):
-        for t in range(n_tx):
-            value = line[0, c, t]
+    for t in range(n_tx):
+        for step in range(1, n_lines):
+            other, place = along(step)
+            pltpu.make_async_remote_copy(
+                src_ref=line.at[other, t],
+                dst_ref=line.at[other, t],
+                send_sem=send2.at[t, step],
+                recv_sem=recv2.at[t, other],
+                device_id=place,
+                device_id_type=MESH,
+            ).wait_recv()
+        for c in range(piece):
+            value = line[0, t, c]
             for l in range(1, n_lines):
-                value = value + line[l, c, t]
-            table[me * piece + c, t] = jnp.concatenate(split_terms(value, 2), axis=0)
-    for step in range(1, peers):
-        other, place = peer(step)
-        copy = pltpu.make_async_remote_copy(
-            src_ref=table.at[mine],
-            dst_ref=table.at[mine],
-            send_sem=send3.at[step],
-            recv_sem=recv3.at[me],
-            device_id=place,
-            device_id_type=MESH,
-        )
-        copy.start()
-        copies.append(copy)
-    for step in range(1, peers):
-        other, place = peer(step)
-        theirs = pl.ds(other * piece, piece)
-        pltpu.make_async_remote_copy(
-            src_ref=table.at[theirs],
-            dst_ref=table.at[theirs],
-            send_sem=send3.at[step],
-            recv_sem=recv3.at[other],
-            device_id=place,
-            device_id_type=MESH,
-        ).wait_recv()
+                value = value + line[l, t, c]
+            tables[t][me * piece + c] = jnp.concatenate(split_terms(value, 2), axis=0)
+        for step in range(1, peers):
+            other, place = peer(step)
+            copy = pltpu.make_async_remote_copy(
+                src_ref=tables[t].at[mine],
+                dst_ref=tables[t].at[mine],
+                send_sem=send3.at[t, step],
+                recv_sem=recv3.at[t, me],
+                device_id=place,
+                device_id_type=MESH,
+            )
+            copy.start()
+            copies.append(copy)
 
     row_ids = lax.broadcasted_iota(jnp.int32, (row_blocks, LANES), 0)
     acc = jnp.zeros((row_blocks, LANES), F32)
     for t in range(n_tx):
         panel_loads[t].wait()
+        for step in range(1, peers):
+            other, place = peer(step)
+            theirs = pl.ds(other * piece, piece)
+            pltpu.make_async_remote_copy(
+                src_ref=tables[t].at[theirs],
+                dst_ref=tables[t].at[theirs],
+                send_sem=send3.at[t, step],
+                recv_sem=recv3.at[t, other],
+                device_id=place,
+                device_id_type=MESH,
+            ).wait_recv()
 
         def some_slots(turn, acc, t=t):
             for u in range(unroll):
                 k = turn * unroll + u
                 slot = grp * width + k
                 r = rows[t, 0, slot]
-                signal = table[columns[t, 0, slot], t]
+                signal = tables[t][columns[t, 0, slot]]
                 both = lax.dot_general(
                     signal,
                     panels_v[t, k],
@@ -281,7 +282,7 @@
     peers = plane * n_grp
     piece = n_blocks // peers
     assert block == LANES and piece * peers == n_blocks and plane * n_lines == n_slab
-    unroll = min(8, width)
+    unroll = min(16, width)
     dims = (n_grp, plane, n_lines, n_tx, n_win, piece, width, unroll)
     vmem = pl.BlockSpec(memory_space=pltpu.VMEM)
     smem = pl.BlockSpec(memory_space=pltpu.SMEM)
@@ -297,18 +298,18 @@
             pltpu.VMEM((n_tx, width, block, block), BF16),
             pltpu.VMEM((peers, piece, n_win, LANES), F32),
             pltpu.VMEM((peers, piece, n_win, LANES), F32),
-            pltpu.VMEM((n_lines, piece, n_tx, n_win, LANES), F32),
-            pltpu.VMEM((n_blocks, n_tx, 2 * n_win, LANES), BF16),
+            pltpu.VMEM((n_lines, n_tx, piece, n_win, LANES), F32),
+            [pltpu.VMEM((n_blocks, 2 * n_win, LANES), BF16)] * n_tx,
             pltpu.VMEM((row_blocks, n_win, LANES), F32),
             pltpu.VMEM((n_grp, row_blocks, LANES), F32),
             dma((peers,)),
             dma((n_tx,)),
             dma((peers,)),
             dma((peers,)),
-            dma((n_lines,)),
-            dma((n_lines,)),
-            dma((peers,)),
-            dma((peers,)),
+            dma((n_tx, n_lines)),
+            dma((n_tx, n_lines)),
+            dma((n_tx, peers)),
+            dma((n_tx, peers)),
             dma((n_grp,)),
             dma((n_grp,)),
         ],

time: 27.7 us -> 24.8 us (0.90)
  Pallas kernels: 26.2 us -> 23.3 us
    pallas_call x1, Pallas kernels: 26.2 us -> 23.3 us  [per_device(): pl.pallas_call(functools.partial(kernel, dims), out_shape=jax.ShapeDtypeS...]
where the time goes in v2:
time: 24.8 us; the launch traced here: 24.6 us
  Pallas kernels  23.3 us (94%)
  local copies, waits for them, and re-layouts  1.26 us (5%)
    pallas_call x1, Pallas kernels, per_device(): pl.pallas_call(functools.partial(kernel, dims), out_shape=jax.ShapeDtypeS...  23.3 us
    unnamed x1, local copies, waits for them, and re-layouts  1.26 us

profile of v2, /device:TPU:0, one launch (start us, length us, event | category | flops | bytes accessed | tf_op | source)
XLA Modules:
  0.0 24.6 jit_solution(2469053834681430438)
XLA Ops:
  0.0 23.3 %beamform.1 = f32[4,128]{1,0:T(4,128)} custom-call(bf16[1,512,2048]{2,1,0:T(8,128)(2,1)} %echo.1, bf16[1,3,32,128,128]{4,3,2,1,0:T(8,128)(2,1)} %panels.1, f32[16,512]{1,0:T(8,128)} %apod.1, s32[8,128]{1,0:T(8,128)} %bitcast.5, s32[3]{0:T(128)} %acquirer.1, s32[1,3]{1,0:T(1,128)} %counts.1, s32[3,1,64]{2,1,0:T(1,128)} %bitcast.6, s32[3,1,64]{2,1,0:T(1,128)} %bitcast.7), custom_call_target="tpu_custom_call" | custom-call | tf_op jit(solution)/shard_map/beamform/pallas_call | solution.py:291
  23.3 1.3 %copy.10 = f32[512]{0:T(512)} copy(f32[512]{0:T(512)} %bitcast.4) | data formatting | bytes 4096

commit v3 on v2

--- a/solution.py
+++ b/solution.py
@@ -20,6 +20,31 @@
         terms.append(term)
         x = x - term.astype(F32)
     return terms
+
+
+STEPS = 32700.0
+FINEST = 16.0
+
+
+def coded(values):
+    lanes = lax.broadcasted_iota(jnp.int32, values[0].shape, 1)
+    logs = jnp.zeros(values[0].shape, F32)
+    tiles = []
+    for number, value in enumerate(values):
+        top = jnp.max(jnp.abs(value), axis=1, keepdims=True)
+        top = jnp.broadcast_to(jnp.maximum(top, 2.0**-120), value.shape)
+        log = jnp.ceil(jnp.log2(top) * FINEST)
+        tiles.append(jnp.round(value * jnp.exp2(log * (-1.0 / FINEST)) * STEPS))
+        logs = jnp.where(lanes == number, log, logs)
+    return tiles, logs
+
+
+def to_16(x):
+    return x.astype(jnp.int32).astype(jnp.int16)
+
+
+def from_16(x):
+    return x.astype(jnp.int32).astype(F32)
 
 
 def kernel(
@@ -38,6 +63,7 @@
     own,
     parts,
     line,
+    shares,
     tables,
     onehot,
     sums,
@@ -139,18 +165,35 @@
             for g in range(1, n_grp):
                 total = total + parts[q * n_grp + g, c]
             records.append(total)
-    for t in range(n_tx):
+    values = []
+    held = []
+    for t in range(n_tx):
+        holder = jnp.full((n_win, LANES), acquirer[t], jnp.int32) - level * plane
+        held.append((holder >= 0) & (holder < plane))
         for c in range(piece):
             value = jnp.zeros((n_win, LANES), F32)
             for q in range(plane):
-                hit = jnp.full((n_win, LANES), acquirer[t], jnp.int32) == level * plane + q
-                value = value + jnp.where(hit, records[c * plane + q], 0.0)
-            line[level, t, c] = value
+                value = jnp.where(holder == q, records[c * plane + q], value)
+            values.append(value)
+    tiles, logs = coded(values)
+    lanes = lax.broadcasted_iota(jnp.int32, (n_win, LANES), 1)
+    kept = jnp.zeros((n_win, LANES), F32)
+    for t in range(n_tx):
+        inside = (lanes >= t * piece) & (lanes < (t + 1) * piece)
+        kept = kept + jnp.where(inside & held[t], logs, 0.0)
+    line[level, 0] = to_16(kept)
+
+    def span_of(t):
+        return pl.ds(0, piece + 1) if t == 0 else pl.ds(1 + t * piece, piece)
+
+    for t in range(n_tx):
+        for c in range(piece):
+            line[level, 1 + t * piece + c] = to_16(tiles[t * piece + c])
         for step in range(1, n_lines):
             other, place = along(step)
             copy = pltpu.make_async_remote_copy(
-                src_ref=line.at[level, t],
-                dst_ref=line.at[level, t],
+                src_ref=line.at[level, span_of(t)],
+                dst_ref=line.at[level, span_of(t)],
                 send_sem=send2.at[t, step],
                 recv_sem=recv2.at[t, level],
                 device_id=place,
@@ -159,28 +202,28 @@
             copy.start()
             copies.append(copy)
 
-    mine = pl.ds(me * piece, piece)
     for t in range(n_tx):
         for step in range(1, n_lines):
             other, place = along(step)
             pltpu.make_async_remote_copy(
-                src_ref=line.at[other, t],
-                dst_ref=line.at[other, t],
+                src_ref=line.at[other, span_of(t)],
+                dst_ref=line.at[other, span_of(t)],
                 send_sem=send2.at[t, step],
                 recv_sem=recv2.at[t, other],
                 device_id=place,
                 device_id_type=MESH,
             ).wait_recv()
-        for c in range(piece):
-            value = line[0, t, c]
+        first = 0 if t == 0 else 1 + t * piece
+        for c in range(shares[t].shape[1]):
+            value = line[0, first + c].astype(jnp.int32)
             for l in range(1, n_lines):
-                value = value + line[l, t, c]
-            tables[t][me * piece + c] = jnp.concatenate(split_terms(value, 2), axis=0)
+                value = value + line[l, first + c].astype(jnp.int32)
+            shares[t][me, c] = value.astype(jnp.int16)
         for step in range(1, peers):
             other, place = peer(step)
             copy = pltpu.make_async_remote_copy(
-                src_ref=tables[t].at[mine],
-                dst_ref=tables[t].at[mine],
+                src_ref=shares[t].at[me],
+                dst_ref=shares[t].at[me],
                 send_sem=send3.at[t, step],
                 recv_sem=recv3.at[t, me],
                 device_id=place,
@@ -195,15 +238,24 @@
         panel_loads[t].wait()
         for step in range(1, peers):
             other, place = peer(step)
-            theirs = pl.ds(other * piece, piece)
             pltpu.make_async_remote_copy(
-                src_ref=tables[t].at[theirs],
-                dst_ref=tables[t].at[theirs],
+                src_ref=shares[t].at[other],
+                dst_ref=shares[t].at[other],
                 send_sem=send3.at[t, step],
                 recv_sem=recv3.at[t, other],
                 device_id=place,
                 device_id_type=MESH,
             ).wait_recv()
+        if t == 0:
+            scales = [
+                jnp.exp2(from_16(shares[0][p, 0]) * (1.0 / FINEST)) * (1.0 / STEPS)
+                for p in range(peers)
+            ]
+        for p in range(peers):
+            for c in range(piece):
+                lane = t * piece + c
+                value = from_16(shares[t][p, c + (t == 0)]) * scales[p][:, lane : lane + 1]
+                tables[t][p * piece + c] = jnp.concatenate(split_terms(value, 2), axis=0)
 
         def some_slots(turn, acc, t=t):
             for u in range(unroll):
@@ -298,7 +350,11 @@
             pltpu.VMEM((n_tx, width, block, block), BF16),
             pltpu.VMEM((peers, piece, n_win, LANES), F32),
             pltpu.VMEM((peers, piece, n_win, LANES), F32),
-            pltpu.VMEM((n_lines, n_tx, piece, n_win, LANES), F32),
+            pltpu.VMEM((n_lines, n_tx * piece + 1, n_win, LANES), jnp.int16),
+            [
+                pltpu.VMEM((peers, piece + (t == 0), n_win, LANES), jnp.int16)
+                for t in range(n_tx)
+            ],
             [pltpu.VMEM((n_blocks, 2 * n_win, LANES), BF16)] * n_tx,
             pltpu.VMEM((row_blocks, n_win, LANES), F32),
             pltpu.VMEM((n_grp, row_blocks, LANES), F32),

time: 24.8 us -> 24.4 us (0.984)
  Pallas kernels: 23.3 us -> 22.9 us
    pallas_call x1, Pallas kernels: 23.3 us -> 22.9 us  [per_device(): pl.pallas_call(functools.partial(kernel, dims), out_shape=jax.ShapeDtypeS...]
where the time goes in v3:
time: 24.4 us; the launch traced here: 24.2 us
  Pallas kernels  22.9 us (94%)
  local copies, waits for them, and re-layouts  1.26 us (5%)
    pallas_call x1, Pallas kernels, per_device(): pl.pallas_call(functools.partial(kernel, dims), out_shape=jax.ShapeDtypeS...  22.9 us
    unnamed x1, local copies, waits for them, and re-layouts  1.26 us

profile of v3, /device:TPU:0, one launch (start us, length us, event | category | flops | bytes accessed | tf_op | source)
XLA Modules:
  0.0 24.2 jit_solution(17325454239406343503)
XLA Ops:
  0.0 22.9 %beamform.1 = f32[4,128]{1,0:T(4,128)} custom-call(bf16[1,512,2048]{2,1,0:T(8,128)(2,1)} %echo.1, bf16[1,3,32,128,128]{4,3,2,1,0:T(8,128)(2,1)} %panels.1, f32[16,512]{1,0:T(8,128)} %apod.1, s32[8,128]{1,0:T(8,128)} %bitcast.5, s32[3]{0:T(128)} %acquirer.1, s32[1,3]{1,0:T(1,128)} %counts.1, s32[3,1,64]{2,1,0:T(1,128)} %bitcast.6, s32[3,1,64]{2,1,0:T(1,128)} %bitcast.7), custom_call_target="tpu_custom_call" | custom-call | tf_op jit(solution)/shard_map/beamform/pallas_call | solution.py:343
  22.9 1.3 %copy.10 = f32[512]{0:T(512)} copy(f32[512]{0:T(512)} %bitcast.4) | data formatting | bytes 4096

commit v4 on v2

--- a/solution.py
+++ b/solution.py
@@ -87,7 +87,6 @@
     panel_loads = []
     for t in range(n_tx):
         load = pltpu.make_async_copy(panels.at[0, t], panels_v.at[t], panel_sem.at[t])
-        load.start()
         panel_loads.append(load)
 
     row_blocks = windows.shape[0]
@@ -100,27 +99,34 @@
     pl.semaphore_wait(barrier, peers - 1 + n_lines - 1)
 
     copies = []
-    for number, part in enumerate(order):
-        loads[number].wait()
-        terms = jnp.dot(weights, echo_v[number], preferred_element_type=F32)
-        value = terms[:n_win] + terms[n_win : 2 * n_win] + terms[2 * n_win :]
-        for c in range(piece):
-            chunk = value[:, c * LANES : (c + 1) * LANES]
-            if number == peers - 1:
-                parts[me, c] = chunk
-            else:
-                own[number, c] = chunk
-        if number < peers - 1:
-            copy = pltpu.make_async_remote_copy(
-                src_ref=own.at[number],
-                dst_ref=parts.at[me],
-                send_sem=send1.at[number],
-                recv_sem=recv1.at[me],
-                device_id=peer(number + 1)[1],
-                device_id_type=MESH,
-            )
-            copy.start()
-            copies.append(copy)
+    half = peers // 2
+    for group in (range(half), range(half, peers)):
+        for number in group:
+            loads[number].wait()
+        if group[-1] == peers - 1:
+            for load in panel_loads:
+                load.start()
+        for number in group:
+            terms = jnp.dot(weights, echo_v[number], preferred_element_type=F32)
+            value = terms[:n_win] + terms[n_win : 2 * n_win] + terms[2 * n_win :]
+            for c in range(piece):
+                chunk = value[:, c * LANES : (c + 1) * LANES]
+                if number == peers - 1:
+                    parts[me, c] = chunk
+                else:
+                    own[number, c] = chunk
+        for number in group:
+            if number < peers - 1:
+                copy = pltpu.make_async_remote_copy(
+                    src_ref=own.at[number],
+                    dst_ref=parts.at[me],
+                    send_sem=send1.at[number],
+                    recv_sem=recv1.at[me],
+                    device_id=peer(number + 1)[1],
+                    device_id_type=MESH,
+                )
+                copy.start()
+                copies.append(copy)
     for step in range(1, peers):
         other, place = peer(step)
         pltpu.make_async_remote_copy(
@@ -206,21 +212,25 @@
             ).wait_recv()
 
         def some_slots(turn, acc, t=t):
-            for u in range(unroll):
-                k = turn * unroll + u
-                slot = grp * width + k
-                r = rows[t, 0, slot]
-                signal = tables[t][columns[t, 0, slot]]
+            for pair in range(unroll // 2):
+                first = turn * unroll + 2 * pair
+                signals = [
+                    tables[t][columns[t, 0, grp * width + first + i]] for i in range(2)
+                ]
                 both = lax.dot_general(
-                    signal,
-                    panels_v[t, k],
+                    jnp.concatenate(signals, axis=0),
+                    panels_v[t, pl.ds(first, 2)].reshape(2 * LANES, LANES),
                     (((1,), (1,)), ((), ())),
                     preferred_element_type=F32,
                 )
-                value = (both[:n_win] + both[n_win:]) * onehot[r]
-                value = jnp.sum(value, axis=0, keepdims=True)
-                target = jnp.where(slot < counts[0, t], r, -1)
-                acc = acc + jnp.where(row_ids == target, value, 0.0)
+                for i in range(2):
+                    slot = grp * width + first + i
+                    r = rows[t, 0, slot]
+                    own_part = both[2 * n_win * i :, i * LANES : (i + 1) * LANES]
+                    value = (own_part[:n_win] + own_part[n_win : 2 * n_win]) * onehot[r]
+                    value = jnp.sum(value, axis=0, keepdims=True)
+                    target = jnp.where(slot < counts[0, t], r, -1)
+                    acc = acc + jnp.where(row_ids == target, value, 0.0)
             return acc
 
         acc = lax.fori_loop(0, width // unroll, some_slots, acc)

time: 24.8 us -> 24.1 us (0.972)
  Pallas kernels: 23.3 us -> 22.6 us
    pallas_call x1, Pallas kernels: 23.3 us -> 22.6 us  [per_device(): pl.pallas_call(functools.partial(kernel, dims), out_shape=jax.ShapeDtypeS...]
where the time goes in v4:
time: 24.1 us; the launch traced here: 23.9 us
  Pallas kernels  22.6 us (94%)
  local copies, waits for them, and re-layouts  1.26 us (5%)
    pallas_call x1, Pallas kernels, per_device(): pl.pallas_call(functools.partial(kernel, dims), out_shape=jax.ShapeDtypeS...  22.6 us
    unnamed x1, local copies, waits for them, and re-layouts  1.26 us

profile of v4, /device:TPU:0, one launch (start us, length us, event | category | flops | bytes accessed | tf_op | source)
XLA Modules:
  0.0 23.9 jit_solution(2667909285978127423)
XLA Ops:
  0.0 22.6 %beamform.1 = f32[4,128]{1,0:T(4,128)} custom-call(bf16[1,512,2048]{2,1,0:T(8,128)(2,1)} %echo.1, bf16[1,3,32,128,128]{4,3,2,1,0:T(8,128)(2,1)} %panels.1, f32[16,512]{1,0:T(8,128)} %apod.1, s32[8,128]{1,0:T(8,128)} %bitcast.5, s32[3]{0:T(128)} %acquirer.1, s32[1,3]{1,0:T(1,128)} %counts.1, s32[3,1,64]{2,1,0:T(1,128)} %bitcast.6, s32[3,1,64]{2,1,0:T(1,128)} %bitcast.7), custom_call_target="tpu_custom_call" | custom-call | tf_op jit(solution)/shard_map/beamform/pallas_call | solution.py:301
  22.6 1.3 %copy.10 = f32[512]{0:T(512)} copy(f32[512]{0:T(512)} %bitcast.4) | data formatting | bytes 4096

commit v5 on v4

--- a/solution.py
+++ b/solution.py
@@ -26,13 +26,20 @@
     dims,
     echo,
     panels,
+    apod_in,
+    windows_in,
+    acquirer_in,
+    counts_in,
+    rows_in,
+    columns_in,
+    image,
     apod,
     windows,
     acquirer,
     counts,
     rows,
     columns,
-    image,
+    small_sem,
     echo_v,
     panels_v,
     own,
@@ -77,6 +84,20 @@
     for step in range(1, n_lines):
         pl.semaphore_signal(barrier, inc=1, device_id=along(step)[1], device_id_type=MESH)
 
+    small = [
+        pltpu.make_async_copy(source, target, small_sem.at[number])
+        for number, (source, target) in enumerate(
+            (
+                (apod_in, apod),
+                (acquirer_in, acquirer),
+                (windows_in, windows),
+                (counts_in, counts),
+                (rows_in, rows),
+                (columns_in, columns),
+            )
+        )
+    ]
+    small[0].start()
     order = [lax.rem(me + step, peers) for step in range(1, peers + 1)]
     loads = []
     for number, part in enumerate(order):
@@ -89,11 +110,10 @@
         load = pltpu.make_async_copy(panels.at[0, t], panels_v.at[t], panel_sem.at[t])
         panel_loads.append(load)
 
-    row_blocks = windows.shape[0]
-    for r in range(row_blocks):
-        ids = lax.broadcasted_iota(jnp.int32, (n_win, LANES), 0)
-        onehot[r] = jnp.where(ids == windows[r : r + 1, :], 1.0, 0.0).astype(F32)
-
+    for load in small[1:]:
+        load.start()
+
+    small[0].wait()
     weights = jnp.concatenate(split_terms(apod[...], 3), axis=0)
 
     pl.semaphore_wait(barrier, peers - 1 + n_lines - 1)
@@ -127,6 +147,13 @@
                 )
                 copy.start()
                 copies.append(copy)
+    for load in small[1:]:
+        load.wait()
+    row_blocks = windows.shape[0]
+    for r in range(row_blocks):
+        ids = lax.broadcasted_iota(jnp.int32, (n_win, LANES), 0)
+        onehot[r] = jnp.where(ids == windows[r : r + 1, :], 1.0, 0.0).astype(F32)
+
     for step in range(1, peers):
         other, place = peer(step)
         pltpu.make_async_remote_copy(
@@ -295,15 +322,21 @@
     unroll = min(16, width)
     dims = (n_grp, plane, n_lines, n_tx, n_win, piece, width, unroll)
     vmem = pl.BlockSpec(memory_space=pltpu.VMEM)
-    smem = pl.BlockSpec(memory_space=pltpu.SMEM)
     hbm = pl.BlockSpec(memory_space=pltpu.HBM)
     dma = pltpu.SemaphoreType.DMA
     result = pl.pallas_call(
         functools.partial(kernel, dims),
         out_shape=jax.ShapeDtypeStruct((row_blocks // n_grp, LANES), F32),
-        in_specs=[hbm, hbm, vmem, vmem, smem, smem, smem, smem],
+        in_specs=[hbm] * 8,
         out_specs=vmem,
         scratch_shapes=[
+            pltpu.VMEM(apodization.shape, F32),
+            pltpu.VMEM((row_blocks, block), jnp.int32),
+            pltpu.SMEM(acquirer.shape, jnp.int32),
+            pltpu.SMEM(block_count.shape, jnp.int32),
+            pltpu.SMEM((n_tx, 1, block_rows.shape[2]), jnp.int32),
+            pltpu.SMEM((n_tx, 1, block_columns.shape[2]), jnp.int32),
+            dma((6,)),
             pltpu.VMEM((peers, channels, piece * LANES), BF16),
             pltpu.VMEM((n_tx, width, block, block), BF16),
             pltpu.VMEM((peers, piece, n_win, LANES), F32),

time: 24.1 us -> 23.2 us (0.963)
  Pallas kernels: 22.6 us -> 21.7 us
    pallas_call x1, Pallas kernels: 22.6 us -> 21.7 us  [per_device(): pl.pallas_call(functools.partial(kernel, dims), out_shape=jax.ShapeDtypeS...]
where the time goes in v5:
time: 23.2 us; the launch traced here: 23 us
  Pallas kernels  21.7 us (94%)
  local copies, waits for them, and re-layouts  1.26 us (5%)
    pallas_call x1, Pallas kernels, per_device(): pl.pallas_call(functools.partial(kernel, dims), out_shape=jax.ShapeDtypeS...  21.7 us
    unnamed x1, local copies, waits for them, and re-layouts  1.26 us

profile of v5, /device:TPU:0, one launch (start us, length us, event | category | flops | bytes accessed | tf_op | source)
XLA Modules:
  0.0 23.0 jit_solution(4962646468945919232)
XLA Ops:
  0.0 21.7 %beamform.1 = f32[4,128]{1,0:T(4,128)} custom-call(bf16[1,512,2048]{2,1,0:T(8,128)(2,1)} %echo.1, bf16[1,3,32,128,128]{4,3,2,1,0:T(8,128)(2,1)} %panels.1, f32[16,512]{1,0:T(8,128)} %apod_in.1, s32[8,128]{1,0:T(8,128)} %bitcast.5, s32[3]{0:T(128)} %acquirer_in.1, s32[1,3]{1,0:T(1,128)} %counts_in.1, s32[3,1,64]{2,1,0:T(1,128)} %bitcast.6, s32[3,1,64]{2,1,0:T(1,128)} %bitcast.7), custom_call_target="tpu_custom_call" | custom-call | tf_op jit(solution)/shard_map/beamform/pallas_call | solution.py:327
  21.8 1.3 %copy.10 = f32[512]{0:T(512)} copy(f32[512]{0:T(512)} %bitcast.4) | data formatting | bytes 4096

commit v6 on v5

--- a/solution.py
+++ b/solution.py
@@ -1,4 +1,5 @@
 import functools
+import math
 
 import jax
 import jax.numpy as jnp
@@ -20,6 +21,14 @@
         terms.append(term)
         x = x - term.astype(F32)
     return terms
+
+
+def each(low, high, step):
+    def body(i, carry):
+        step(i)
+        return carry
+
+    lax.fori_loop(low, high, body, 0)
 
 
 def kernel(
@@ -79,10 +88,12 @@
         return other, (slab, other)
 
     barrier = pltpu.get_barrier_semaphore()
-    for step in range(1, peers):
-        pl.semaphore_signal(barrier, inc=1, device_id=peer(step)[1], device_id_type=MESH)
-    for step in range(1, n_lines):
-        pl.semaphore_signal(barrier, inc=1, device_id=along(step)[1], device_id_type=MESH)
+
+    def greet(place):
+        pl.semaphore_signal(barrier, inc=1, device_id=place, device_id_type=MESH)
+
+    each(1, peers, lambda step: greet(peer(step)[1]))
+    each(1, n_lines, lambda step: greet(along(step)[1]))
 
     small = [
         pltpu.make_async_copy(source, target, small_sem.at[number])
@@ -98,17 +109,24 @@
         )
     ]
     small[0].start()
-    order = [lax.rem(me + step, peers) for step in range(1, peers + 1)]
-    loads = []
-    for number, part in enumerate(order):
+    turns = math.gcd(peers, 4)
+    chunks = peers // turns
+
+    def record_load(number):
+        part = lax.rem(me + number + 1, peers)
         cut = pl.ds(pl.multiple_of(part * span, span), span)
-        load = pltpu.make_async_copy(echo.at[0, :, cut], echo_v.at[number], echo_sem.at[number])
-        load.start()
-        loads.append(load)
-    panel_loads = []
-    for t in range(n_tx):
-        load = pltpu.make_async_copy(panels.at[0, t], panels_v.at[t], panel_sem.at[t])
-        panel_loads.append(load)
+        return pltpu.make_async_copy(
+            echo.at[0, :, cut], echo_v.at[number], echo_sem.at[number]
+        )
+
+    def send_load(number):
+        record_load(number).start()
+
+    each(0, peers, send_load)
+    panel_loads = [
+        pltpu.make_async_copy(panels.at[0, t], panels_v.at[t], panel_sem.at[t])
+        for t in range(n_tx)
+    ]
 
     for load in small[1:]:
         load.start()
@@ -118,35 +136,38 @@
 
     pl.semaphore_wait(barrier, peers - 1 + n_lines - 1)
 
-    copies = []
-    half = peers // 2
-    for group in (range(half), range(half, peers)):
-        for number in group:
-            loads[number].wait()
-        if group[-1] == peers - 1:
-            for load in panel_loads:
-                load.start()
-        for number in group:
+    def send_piece(step):
+        other, place = peer(step)
+        return pltpu.make_async_remote_copy(
+            src_ref=own.at[step - 1],
+            dst_ref=parts.at[me],
+            send_sem=send1.at[step - 1],
+            recv_sem=recv1.at[me],
+            device_id=place,
+            device_id_type=MESH,
+        )
+
+    def some_chunks(turn):
+        for u in range(chunks):
+            record_load(turn * chunks + u).wait()
+        for u in range(chunks):
+            number = turn * chunks + u
             terms = jnp.dot(weights, echo_v[number], preferred_element_type=F32)
             value = terms[:n_win] + terms[n_win : 2 * n_win] + terms[2 * n_win :]
             for c in range(piece):
-                chunk = value[:, c * LANES : (c + 1) * LANES]
-                if number == peers - 1:
-                    parts[me, c] = chunk
-                else:
-                    own[number, c] = chunk
-        for number in group:
-            if number < peers - 1:
-                copy = pltpu.make_async_remote_copy(
-                    src_ref=own.at[number],
-                    dst_ref=parts.at[me],
-                    send_sem=send1.at[number],
-                    recv_sem=recv1.at[me],
-                    device_id=peer(number + 1)[1],
-                    device_id_type=MESH,
-                )
-                copy.start()
-                copies.append(copy)
+                own[number, c] = value[:, c * LANES : (c + 1) * LANES]
+        for u in range(chunks):
+            number = turn * chunks + u
+
+            @pl.when(number < peers - 1)
+            def _():
+                send_piece(number + 1).start()
+
+    each(0, turns, some_chunks)
+    parts[me] = own[peers - 1]
+    for load in panel_loads:
+        load.start()
+    copies = []
     for load in small[1:]:
         load.wait()
     row_blocks = windows.shape[0]
@@ -154,7 +175,8 @@
         ids = lax.broadcasted_iota(jnp.int32, (n_win, LANES), 0)
         onehot[r] = jnp.where(ids == windows[r : r + 1, :], 1.0, 0.0).astype(F32)
 
-    for step in range(1, peers):
+
+    def take_piece(step):
         other, place = peer(step)
         pltpu.make_async_remote_copy(
             src_ref=own.at[0],
@@ -164,6 +186,8 @@
             device_id=place,
             device_id_type=MESH,
         ).wait_recv()
+
+    each(1, peers, take_piece)
 
     records = []
     for c in range(piece):
@@ -192,7 +216,18 @@
             copy.start()
             copies.append(copy)
 
-    mine = pl.ds(me * piece, piece)
+    def share_copy(t, step, owner):
+        other, place = peer(step)
+        rows_of = pl.ds((me if owner is me else other) * piece, piece)
+        return pltpu.make_async_remote_copy(
+            src_ref=tables[t].at[rows_of],
+            dst_ref=tables[t].at[rows_of],
+            send_sem=send3.at[t, step],
+            recv_sem=recv3.at[t, me if owner is me else other],
+            device_id=place,
+            device_id_type=MESH,
+        )
+
     for t in range(n_tx):
         for step in range(1, n_lines):
             other, place = along(step)
@@ -209,34 +244,13 @@
             for l in range(1, n_lines):
                 value = value + line[l, t, c]
             tables[t][me * piece + c] = jnp.concatenate(split_terms(value, 2), axis=0)
-        for step in range(1, peers):
-            other, place = peer(step)
-            copy = pltpu.make_async_remote_copy(
-                src_ref=tables[t].at[mine],
-                dst_ref=tables[t].at[mine],
-                send_sem=send3.at[t, step],
-                recv_sem=recv3.at[t, me],
-                device_id=place,
-                device_id_type=MESH,
-            )
-            copy.start()
-            copies.append(copy)
+        each(1, peers, lambda step, t=t: share_copy(t, step, me).start())
 
     row_ids = lax.broadcasted_iota(jnp.int32, (row_blocks, LANES), 0)
     acc = jnp.zeros((row_blocks, LANES), F32)
     for t in range(n_tx):
         panel_loads[t].wait()
-        for step in range(1, peers):
-            other, place = peer(step)
-            theirs = pl.ds(other * piece, piece)
-            pltpu.make_async_remote_copy(
-                src_ref=tables[t].at[theirs],
-                dst_ref=tables[t].at[theirs],
-                send_sem=send3.at[t, step],
-                recv_sem=recv3.at[t, other],
-                device_id=place,
-                device_id_type=MESH,
-            ).wait_recv()
+        each(1, peers, lambda step, t=t: share_copy(t, step, None).wait_recv())
 
         def some_slots(turn, acc, t=t):
             for pair in range(unroll // 2):
@@ -295,6 +309,9 @@
     image[...] = result
     for copy in copies:
         copy.wait_send()
+    each(1, peers, lambda step: send_piece(step).wait_send())
+    for t in range(n_tx):
+        each(1, peers, lambda step, t=t: share_copy(t, step, me).wait_send())
 
 
 def per_device(

time: 23.2 us -> 23.3 us (level)
  no operation moved by 1% of the time
where the time goes in v6:
time: 23.3 us; the launch traced here: 23.2 us
  Pallas kernels  21.9 us (94%)
  local copies, waits for them, and re-layouts  1.26 us (5%)
    pallas_call x1, Pallas kernels, per_device(): pl.pallas_call(functools.partial(kernel, dims), out_shape=jax.ShapeDtypeS...  21.9 us
    unnamed x1, local copies, waits for them, and re-layouts  1.26 us

profile of v6, /device:TPU:0, one launch (start us, length us, event | category | flops | bytes accessed | tf_op | source)
XLA Modules:
  0.0 23.2 jit_solution(5707509688361243237)
XLA Ops:
  0.0 21.9 %beamform.1 = f32[4,128]{1,0:T(4,128)} custom-call(bf16[1,512,2048]{2,1,0:T(8,128)(2,1)} %echo.1, bf16[1,3,32,128,128]{4,3,2,1,0:T(8,128)(2,1)} %panels.1, f32[16,512]{1,0:T(8,128)} %apod_in.1, s32[8,128]{1,0:T(8,128)} %bitcast.5, s32[3]{0:T(128)} %acquirer_in.1, s32[1,3]{1,0:T(1,128)} %counts_in.1, s32[3,1,64]{2,1,0:T(1,128)} %bitcast.6, s32[3,1,64]{2,1,0:T(1,128)} %bitcast.7), custom_call_target="tpu_custom_call" | custom-call | tf_op jit(solution)/shard_map/beamform/pallas_call | solution.py:344
  21.9 1.3 %copy.10 = f32[512]{0:T(512)} copy(f32[512]{0:T(512)} %bitcast.4) | data formatting | bytes 4096

commit v7 on v5

--- a/solution.py
+++ b/solution.py
@@ -42,6 +42,7 @@
     small_sem,
     echo_v,
     panels_v,
+    turned,
     own,
     parts,
     line,
@@ -117,6 +118,18 @@
     weights = jnp.concatenate(split_terms(apod[...], 3), axis=0)
 
     pl.semaphore_wait(barrier, peers - 1 + n_lines - 1)
+
+    def turn_panels(t):
+        panel_loads[t].wait()
+
+        def two_pairs(turn, carry):
+            for i in range(2):
+                pair = 2 * turn + i
+                for j in range(2):
+                    turned[t, pair, :, j * LANES : (j + 1) * LANES] = panels_v[t, 2 * pair + j].T
+            return carry
+
+        lax.fori_loop(0, width // 4, two_pairs, 0)
 
     copies = []
     half = peers // 2
@@ -154,6 +167,7 @@
         ids = lax.broadcasted_iota(jnp.int32, (n_win, LANES), 0)
         onehot[r] = jnp.where(ids == windows[r : r + 1, :], 1.0, 0.0).astype(F32)
 
+    turn_panels(0)
     for step in range(1, peers):
         other, place = peer(step)
         pltpu.make_async_remote_copy(
@@ -191,6 +205,8 @@
             )
             copy.start()
             copies.append(copy)
+
+    turn_panels(1)
 
     mine = pl.ds(me * piece, piece)
     for t in range(n_tx):
@@ -224,8 +240,9 @@
 
     row_ids = lax.broadcasted_iota(jnp.int32, (row_blocks, LANES), 0)
     acc = jnp.zeros((row_blocks, LANES), F32)
+    for t in range(2, n_tx):
+        turn_panels(t)
     for t in range(n_tx):
-        panel_loads[t].wait()
         for step in range(1, peers):
             other, place = peer(step)
             theirs = pl.ds(other * piece, piece)
@@ -244,10 +261,9 @@
                 signals = [
                     tables[t][columns[t, 0, grp * width + first + i]] for i in range(2)
                 ]
-                both = lax.dot_general(
+                both = jnp.dot(
                     jnp.concatenate(signals, axis=0),
-                    panels_v[t, pl.ds(first, 2)].reshape(2 * LANES, LANES),
-                    (((1,), (1,)), ((), ())),
+                    turned[t, turn * (unroll // 2) + pair],
                     preferred_element_type=F32,
                 )
                 for i in range(2):
@@ -339,6 +355,7 @@
             dma((6,)),
             pltpu.VMEM((peers, channels, piece * LANES), BF16),
             pltpu.VMEM((n_tx, width, block, block), BF16),
+            pltpu.VMEM((n_tx, width // 2, block, 2 * block), BF16),
             pltpu.VMEM((peers, piece, n_win, LANES), F32),
             pltpu.VMEM((peers, piece, n_win, LANES), F32),
             pltpu.VMEM((n_lines, n_tx, piece, n_win, LANES), F32),

time: 23.2 us -> 23.1 us (level)
  no operation moved by 1% of the time
where the time goes in v7:
time: 23.1 us; the launch traced here: 22.9 us
  Pallas kernels  21.6 us (94%)
  local copies, waits for them, and re-layouts  1.26 us (5%)
    pallas_call x1, Pallas kernels, per_device(): pl.pallas_call(functools.partial(kernel, dims), out_shape=jax.ShapeDtypeS...  21.6 us
    unnamed x1, local copies, waits for them, and re-layouts  1.26 us

profile of v7, /device:TPU:0, one launch (start us, length us, event | category | flops | bytes accessed | tf_op | source)
XLA Modules:
  0.0 22.9 jit_solution(16738187128090572357)
XLA Ops:
  0.0 21.6 %beamform.1 = f32[4,128]{1,0:T(4,128)} custom-call(bf16[1,512,2048]{2,1,0:T(8,128)(2,1)} %echo.1, bf16[1,3,32,128,128]{4,3,2,1,0:T(8,128)(2,1)} %panels.1, f32[16,512]{1,0:T(8,128)} %apod_in.1, s32[8,128]{1,0:T(8,128)} %bitcast.5, s32[3]{0:T(128)} %acquirer_in.1, s32[1,3]{1,0:T(1,128)} %counts_in.1, s32[3,1,64]{2,1,0:T(1,128)} %bitcast.6, s32[3,1,64]{2,1,0:T(1,128)} %bitcast.7), custom_call_target="tpu_custom_call" | custom-call | tf_op jit(solution)/shard_map/beamform/pallas_call | solution.py:343
  21.7 1.3 %copy.10 = f32[512]{0:T(512)} copy(f32[512]{0:T(512)} %bitcast.4) | data formatting | bytes 4096

commit v8 on v5

--- a/solution.py
+++ b/solution.py
@@ -20,6 +20,10 @@
         terms.append(term)
         x = x - term.astype(F32)
     return terms
+
+
+def far_first(n):
+    return sorted(range(1, n), key=lambda step: abs(2 * step - n))
 
 
 def kernel(
@@ -116,8 +120,6 @@
     small[0].wait()
     weights = jnp.concatenate(split_terms(apod[...], 3), axis=0)
 
-    pl.semaphore_wait(barrier, peers - 1 + n_lines - 1)
-
     copies = []
     half = peers // 2
     for group in (range(half), range(half, peers)):
@@ -135,6 +137,8 @@
                     parts[me, c] = chunk
                 else:
                     own[number, c] = chunk
+        if group[0] == 0:
+            pl.semaphore_wait(barrier, peers - 1 + n_lines - 1)
         for number in group:
             if number < peers - 1:
                 copy = pltpu.make_async_remote_copy(
@@ -209,7 +213,7 @@
             for l in range(1, n_lines):
                 value = value + line[l, t, c]
             tables[t][me * piece + c] = jnp.concatenate(split_terms(value, 2), axis=0)
-        for step in range(1, peers):
+        for step in far_first(peers):
             other, place = peer(step)
             copy = pltpu.make_async_remote_copy(
                 src_ref=tables[t].at[mine],

time: 23.2 us -> 23.1 us (level)
  no operation moved by 1% of the time
where the time goes in v8:
time: 23.1 us; the launch traced here: 22.9 us
  Pallas kernels  21.6 us (94%)
  local copies, waits for them, and re-layouts  1.26 us (5%)
    pallas_call x1, Pallas kernels, per_device(): pl.pallas_call(functools.partial(kernel, dims), out_shape=jax.ShapeDtypeS...  21.6 us
    unnamed x1, local copies, waits for them, and re-layouts  1.26 us

profile of v8, /device:TPU:0, one launch (start us, length us, event | category | flops | bytes accessed | tf_op | source)
XLA Modules:
  0.0 22.9 jit_solution(15088030745340719179)
XLA Ops:
  0.0 21.6 %beamform.1 = f32[4,128]{1,0:T(4,128)} custom-call(bf16[1,512,2048]{2,1,0:T(8,128)(2,1)} %echo.1, bf16[1,3,32,128,128]{4,3,2,1,0:T(8,128)(2,1)} %panels.1, f32[16,512]{1,0:T(8,128)} %apod_in.1, s32[8,128]{1,0:T(8,128)} %bitcast.5, s32[3]{0:T(128)} %acquirer_in.1, s32[1,3]{1,0:T(1,128)} %counts_in.1, s32[3,1,64]{2,1,0:T(1,128)} %bitcast.6, s32[3,1,64]{2,1,0:T(1,128)} %bitcast.7), custom_call_target="tpu_custom_call" | custom-call | tf_op jit(solution)/shard_map/beamform/pallas_call | solution.py:331
  21.6 1.3 %copy.10 = f32[512]{0:T(512)} copy(f32[512]{0:T(512)} %bitcast.4) | data formatting | bytes 4096
